TPU v7x, 1024 devices: a whole 4x8x16 slice. The times are simulated.
1024 devices in a mesh: samp: 16 (over x, z_lo), feat: 64 (over z_hi, y, core).
Axes of the slice: x: 4, y: 8, z: 16 (z_hi: 4, z_lo: 4; z = z_hi * 4 + z_lo), core: 2. Of those that a mesh axis runs over, the one named last changes fastest.
Arguments:
- data: float32 [16384, 16384], P('samp', 'feat'), may hold values from -0.1118034 to 0.1118034, as said below
- targets: float32 [16384, 128], P(('samp', 'feat')), may hold values from -36 to 36
- coef: float32 [16384, 128], P('feat'), may hold values from -6 to 6
- coef_dual: float32 [16384, 128], P('feat'), may hold values from -3 to 3
- tile_coef_dual: float32 [16, 16384, 128], P('samp', 'feat'), may hold values from -3 to 3
- share: float32 [16384, 128], P(('samp', 'feat')), may hold values from -36 to 36
- share_dual: float32 [16384, 128], P('samp'), may hold values from -6 to 6
- tile_share: float32 [64, 16384, 128], P('feat', 'samp'), may hold values from -6 to 6
Outputs:
- coef_out: float32 [16384, 128], P('feat')
- coef_dual_out: float32 [16384, 128], P('feat')
- tile_coef_dual_out: float32 [16, 16384, 128], P('samp', 'feat')
- share_out: float32 [16384, 128], P(('samp', 'feat'))
- share_dual_out: float32 [16384, 128], P('samp')
- tile_share_out: float32 [64, 16384, 128], P('feat', 'samp')
Inputs may be any that keep to these rules, and one draw needn't show every extreme that they name: `data`: independent entries of mean zero and variance 1 / 1280.
All inputs are finite; a program needn't handle non-finite values.
Results may differ from a plain program's by a relative error of at most 0.0001.
Values sent between devices are 32-bit elements; how exact they have to be, the bound alone decides.
A program may use at most 32 MiB of HBM per device.

v0:
```python
import jax
import jax.numpy as jnp
from jax import lax
from jax.sharding import PartitionSpec as P

ITERS = 2
CHEB = 5


cheb_low = 1.0
cheb_high = 3.2
l1_weight = 0.2
huber_width = 4.0


def chebyshev(apply_fn, rhs, start):
    theta = (cheb_high + cheb_low) / 2.0
    delta = (cheb_high - cheb_low) / 2.0
    sigma = theta / delta
    iterate = start
    resid = rhs - apply_fn(iterate)
    search = resid / theta
    rho_old = 1.0 / sigma
    for step in range(CHEB):
        iterate = iterate + search
        if step + 1 < CHEB:
            resid = resid - apply_fn(search)
            rho_new = 1.0 / (2.0 * sigma - rho_old)
            search = rho_new * rho_old * search + 2.0 * rho_new / delta * resid
            rho_old = rho_new
    return iterate


def shards(data, targets, coef, coef_dual, tile_coef_dual, share, share_dual, tile_share):
    high = lax.Precision.HIGHEST
    feat_count = lax.axis_size("feat")
    samp_count = lax.axis_size("samp")
    own_rows = share.shape[0]
    feat_index = lax.axis_index("feat")
    tile_dual = tile_coef_dual[0]
    tile_out = tile_share[0]

    def transpose_mul(vector):
        return jnp.einsum("sf,sk->fk", data, vector, precision=high)

    def forward_mul(vector):
        return jnp.dot(data, vector, precision=high)

    def apply_fn(vector):
        return vector + transpose_mul(forward_mul(vector))

    for sweep in range(ITERS):
        value = coef - coef_dual
        half_coef = value - jnp.clip(value, -l1_weight, l1_weight)
        dual_rows = lax.dynamic_slice_in_dim(share_dual, feat_index * own_rows, own_rows, 0)
        resid_t = share - dual_rows - targets
        half_share = targets + resid_t - jnp.clip(resid_t / 2.0, -huber_width, huber_width)
        start = coef - tile_dual
        rhs = start + transpose_mul(tile_out + share_dual)
        proj_coef = chebyshev(apply_fn, rhs, start)
        proj_share = forward_mul(proj_coef)
        summed = lax.psum(proj_coef, "samp")
        coef_new = (half_coef + summed) / (samp_count + 1)
        whole_sum = lax.psum(proj_share, "feat")
        half_all = lax.all_gather(half_share, "feat", axis=0, tiled=True)
        excess = (half_all - whole_sum) / (feat_count + 1)
        excess_own = lax.dynamic_slice_in_dim(excess, feat_index * own_rows, own_rows, 0)
        share = half_share - excess_own
        tile_out = proj_share + excess
        share_dual = share_dual + excess
        coef_dual = coef_dual + half_coef - coef_new
        tile_dual = tile_dual + proj_coef - coef_new
        coef = coef_new
    return (coef, coef_dual, tile_dual[None], share, share_dual, tile_out[None])


def solution(mesh):
    return jax.shard_map(
        shards,
        mesh=mesh,
        in_specs=(
            P("samp", "feat"),
            P(("samp", "feat"), None),
            P("feat", None),
            P("feat", None),
            P("samp", "feat", None),
            P(("samp", "feat"), None),
            P("samp", None),
            P("feat", "samp", None),
        ),
        out_specs=(
            P("feat", None),
            P("feat", None),
            P("samp", "feat", None),
            P(("samp", "feat"), None),
            P("samp", None),
            P("feat", "samp", None),
        ),
        check_vma=False,
    )
```

profile of v0, /device:TPU:1, one launch (start us, length us, event | category | flops | bytes accessed | tf_op | source)
XLA Modules:
  0.0 1744.8 jit_solution(3817667347253862317)
XLA Ops:
  7.2 1.1 copy.54
  8.3 0.1 copy.56
  8.5 1.2 fusion.53
  9.8 1.0 fusion.25
  10.8 0.6 fusion.24
  11.4 1.2 fusion.33
  12.6 0.6 fusion.22
  13.3 1.2 fusion.50
  14.5 0.6 multiply_add_fusion.4
  15.1 1.2 fusion.54
  16.3 0.6 fusion.18
  17.0 1.2 fusion.35
  18.2 1.3 fusion.26
  19.5 0.0 all-reduce.7.cloned.1.call-start
  19.5 0.8 copy-done.3
  20.4 1.8 convolution_bitcast_fusion.1
  22.2 0.0 all-reduce.9.cloned.1.call-start
  22.2 0.6 copy-done.16
  22.9 118.0 %all_gather.6 = f32[1024,128]{1,0:T(8,128)} all-gather(f32[16,128]{1,0:T(8,128)S(1)} %clamp_subtract_fusion.3), channel_id=1, replica_groups=mesh['samp'=16,'feat'=64] {'feat'}, dimensions={0}, use_global_device_ids=true | all-gather | bytes 532480 | tf_op jit(solution)/shard_map/all_gather | solution.py:65
  140.9 0.1 copy.55
  141.0 53.2 %all-reduce.5.cloned.1.call-done = f32[256,128]{0,1:T(8,128)} async-done(((f32[256,128]{0,1:T(8,128)}), f32[256,128]{0,1:T(8,128)}) %all-reduce.5.cloned.1.call-update) | async-done | bytes 131088 | tf_op jit(solution)/shard_map/psum | solution.py:62
  194.1 0.9 fusion.43
  195.1 2.0 fusion.55
  197.1 680.6 %all-reduce.7.cloned.1.call-done = f32[1024,128]{1,0:T(8,128)} async-done(((f32[1024,128]{1,0:T(8,128)}), f32[1024,128]{1,0:T(8,128)}) %all-reduce.7.cloned.1.call-update) | async-done | bytes 524304 | tf_op jit(solution)/shard_map/psum | solution.py:64
  877.8 1.3 fusion.52
  879.1 1.0 fusion.12
  880.1 0.6 fusion.11
  880.8 1.2 fusion.31
  882.0 0.6 fusion.9
  882.6 1.2 fusion.51
  883.8 0.6 multiply_add_fusion.1
  884.5 1.2 fusion.56
  885.7 0.6 fusion.5
  886.3 1.2 fusion.36
  887.5 1.3 fusion.27
  888.8 0.0 all-reduce.11.cloned.1.call-start
  888.9 0.8 copy-done.7
  889.7 1.8 convolution_bitcast_fusion
  891.6 99.5 %all_gather.7 = f32[1024,128]{1,0:T(8,128)S(1)} all-gather(f32[16,128]{1,0:T(8,128)S(1)} %clamp_subtract_fusion.2), channel_id=1, replica_groups=mesh['samp'=16,'feat'=64] {'feat'}, dimensions={0}, use_global_device_ids=true | all-gather | bytes 532480 | tf_op jit(solution)/shard_map/all_gather | solution.py:65
  991.1 60.3 %all-reduce.9.cloned.1.call-done = f32[256,128]{0,1:T(8,128)} async-done(((f32[256,128]{0,1:T(8,128)}), f32[256,128]{0,1:T(8,128)}) %all-reduce.9.cloned.1.call-update) | async-done | bytes 131088 | tf_op jit(solution)/shard_map/psum | solution.py:62
  1051.4 1.0 subtract_bitcast_fusion
  1052.4 0.8 copy.61
  1053.1 0.8 copy.62
  1053.9 0.8 copy.63
  1054.7 680.2 %all-reduce.11.cloned.1.call-done = f32[1024,128]{1,0:T(8,128)} async-done(((f32[1024,128]{1,0:T(8,128)}), f32[1024,128]{1,0:T(8,128)}) %all-reduce.11.cloned.1.call-update) | async-done | bytes 524304 | tf_op jit(solution)/shard_map/psum | solution.py:64
  1734.9 1.9 add_bitcast_fusion
  1736.8 0.6 dynamic-slice_subtract_fusion
  1737.4 0.8 add.189
  (39 shorter events, 0.3 us)
Async XLA Ops:
  7.2 1.4 copy-start
  7.2 1.2 copy-start.13
  7.2 186.9 %all-reduce.5.cloned.1.call-start = ((), (), s32[]{:S(2)}) async-start(), calls=%async_computation | async-start | bytes 262144 | tf_op jit(solution)/shard_map/psum | solution.py:62
  8.4 185.7 %copy-start.5 = (f32[1,256,128]{1,2,0:T(8,128)}, f32[1,256,128]{1,2,0:T(8,128)S(1)}, u32[]{:S(2)}) copy-start(f32[1,256,128]{1,2,0:T(8,128)S(1)} %copy.56) | copy-start | bytes 393220
  8.5 1.2 copy-start.4
  8.5 1.2 copy-start.12
  19.5 0.9 copy-start.3
  19.5 858.3 %all-reduce.7.cloned.1.call-start = ((), (), s32[]{:S(2)}) async-start(), calls=%async_computation.1 | async-start | bytes 1048576 | tf_op jit(solution)/shard_map/psum | solution.py:64
  22.2 0.7 copy-start.16
  22.2 0.7 copy-start.15
  22.2 1029.2 %all-reduce.9.cloned.1.call-start = ((), (), s32[]{:S(2)}) async-start(), calls=%async_computation.2 | async-start | bytes 262144 | tf_op jit(solution)/shard_map/psum | solution.py:62
  22.9 118.0 %copy-start.14 = (f32[256,128]{1,0:T(8,128)S(1)}, f32[256,128]{1,0:T(8,128)}, u32[]{:S(2)}) copy-start(f32[256,128]{1,0:T(8,128)} %param.11) | copy-start | bytes 393220
  141.0 54.1 %copy-start.9 = (f32[256,128]{0,1:T(8,128)}, f32[256,128]{0,1:T(8,128)S(1)}, u32[]{:S(2)}) copy-start(f32[256,128]{0,1:T(8,128)S(1)} %copy.55) | copy-start | bytes 393220
  197.1 681.9 %copy-start.2 = (f32[1024,128]{1,0:T(8,128)S(1)}, f32[1024,128]{1,0:T(8,128)}, u32[]{:S(2)}) copy-start(f32[1024,128]{1,0:T(8,128)} %convolution_bitcast_fusion.1) | copy-start | bytes 1572868
  879.1 1.1 copy-start.8
  888.8 0.9 copy-start.7
  888.8 846.0 %all-reduce.11.cloned.1.call-start = ((), (), s32[]{:S(2)}) async-start(), calls=%async_computation.3 | async-start | bytes 1048576 | tf_op jit(solution)/shard_map/psum | solution.py:64
  891.5 159.8 %copy-start.6 = (f32[1,256,128]{1,2,0:T(8,128)S(1)}, f32[1,256,128]{1,2,0:T(8,128)}, u32[]{:S(2)}) copy-start(f32[1,256,128]{1,2,0:T(8,128)} %copy-done.5) | copy-start | bytes 393220
  891.6 159.8 %copy-start.10 = (f32[256,128]{0,1:T(8,128)S(1)}, f32[256,128]{0,1:T(8,128)}, u32[]{:S(2)}) copy-start(f32[256,128]{0,1:T(8,128)} %copy-done.9) | copy-start | bytes 393220
  891.6 159.8 %copy-start.11 = (f32[256,128]{0,1:T(8,128)S(1)}, f32[256,128]{0,1:T(8,128)}, u32[]{:S(2)}) copy-start(f32[256,128]{0,1:T(8,128)} %all-reduce.5.cloned.1.call-done) | copy-start | bytes 393220
  1052.4 682.5 %copy-start.1 = (f32[1024,128]{1,0:T(8,128)S(1)}, f32[1024,128]{1,0:T(8,128)}, u32[]{:S(2)}) copy-start(f32[1024,128]{1,0:T(8,128)} %convolution_bitcast_fusion) | copy-start | bytes 1572868
Sparse Core Ops, SparseCore 0:
  19.6 174.4 all-reduce.4
  198.6 679.1 all-reduce.6
  889.0 162.3 all-reduce.8
  1055.7 679.1 all-reduce.10
where the time goes:
time: 1750 us; the launch traced here: 1740 us
  waiting for transfers between devices  1470 us (84%)
  blocking collectives  217 us (12%)
  matrix products  26.1 us (1%)
    psum x2, waiting for transfers between devices, shards(): whole_sum = lax.psum(proj_share, 'feat')  1360 us
    all_gather x2, blocking collectives, shards(): half_all = lax.all_gather(half_share, 'feat', axis=0, tiled=True)  217 us
    psum x2, waiting for transfers between devices, shards(): summed = lax.psum(proj_coef, 'samp')  113 us
  transfers between devices with their start and end apart: 4, of which 4 were waited for; matrix products, arithmetic and copies ran while one was open for 1% of the time, Pallas kernels for 0%

commit v1 on v0

v1 whole, which is shorter than its diff:
```python
import functools

import jax
import jax.numpy as jnp
from jax import lax
from jax.experimental import pallas as pl
from jax.experimental.pallas import tpu as pltpu
from jax.sharding import PartitionSpec as P

ITERS = 2
CHEB = 5

cheb_low = 1.0
cheb_high = 3.2
l1_weight = 0.2
huber_width = 4.0

NX, NL, NH, NY, NC = 4, 4, 4, 8, 2
B = 16
K = 128

MESH = pl.DeviceIdType.MESH
f32 = jnp.float32
bf16 = jnp.bfloat16


def split(v):
    hi = v.astype(bf16)
    return hi, (v - hi.astype(f32)).astype(bf16)


def mul(lhs_hi, lhs_lo, v):
    hi, lo = split(v)
    both = jnp.dot(lhs_hi, jnp.concatenate([hi, lo], axis=1), preferred_element_type=f32)
    return both[:, :K] + both[:, K:] + jnp.dot(lhs_lo, hi, preferred_element_type=f32)


def far_first(n):
    return sorted(range(1, n), key=lambda p: -min(p, n - p))


def body(
    data, targets, coef, cdual, tdual, share, sdual, tshare,
    o_coef, o_cdual, o_tdual, o_share, o_sdual, o_tshare,
    a32, a_hi, a_lo, at_hi, at_lo, gram_hi, gram_lo,
    v_targets, v_coef, v_cdual, v_tdual, v_share, v_sdual, v_tshare,
    ps, pair_in, y_out, y_in, h_out, h_in, exc, zc, x_in, l_out, l_in, cnew,
    load_sem, store_sem, send_sem, recv_sem,
):
    half = NY * NH * B
    rows = NC * half
    feats = NX * NL * B
    s, f = lax.axis_index("samp"), lax.axis_index("feat")
    x, l = s // NL, s % NL
    h, y, c = f // (NY * NC), (f // NC) % NY, f % NC
    other = 1 - c

    def feat_dev(h_, y_, c_):
        return (s, (h_ * NY + y_) * NC + c_)

    def samp_dev(x_, l_):
        return (x_ * NL + l_, f)

    y_order, h_order, x_order, l_order = far_first(NY), far_first(NH), far_first(NX), far_first(NL)

    loads = []

    def load(src, dst):
        copy = pltpu.make_async_copy(src, dst, load_sem.at[len(loads)])
        copy.start()
        loads.append(copy)
        return copy

    data_loads = [load(data.at[k, :, m], a32.at[m, :, k]) for m in range(NC) for k in range(NH)]
    out_loads = [
        load(src.at[k, :, m], dst.at[m, :, k])
        for src, dst in ((tshare, v_tshare), (sdual, v_sdual))
        for m in range(NC)
        for k in range(NH)
    ]
    small_loads = [
        load(coef, v_coef.at[0]),
        load(tdual, v_tdual.at[0]),
        load(cdual, v_cdual.at[0]),
        load(targets, v_targets),
        load(share, v_share),
    ]

    barrier = pltpu.get_barrier_semaphore()
    partners = (
        [feat_dev(h, y, other)]
        + [feat_dev(h, (y + p) % NY, c) for p in range(1, NY)]
        + [feat_dev((h + p) % NH, y, c) for p in range(1, NH)]
        + [samp_dev((x + p) % NX, l) for p in range(1, NX)]
        + [samp_dev(x, (l + p) % NL) for p in range(1, NL)]
    )
    for who in partners:
        pl.semaphore_signal(barrier, inc=1, device_id=who, device_id_type=MESH)

    for copy in data_loads:
        copy.wait()
    a = a32[...].reshape(rows, feats)
    hi, lo = split(a)
    a_hi[...] = hi.reshape(NC, half, feats)
    a_lo[...] = lo.reshape(NC, half, feats)
    hi, lo = split(a.T)
    at_hi[...] = hi
    at_lo[...] = lo
    gram = jnp.zeros((feats, feats), f32)
    for m in range(NC):
        cols = slice(m * half, (m + 1) * half)
        both = jnp.dot(
            at_hi[:, cols], jnp.concatenate([a_hi[m], a_lo[m]], axis=1), preferred_element_type=f32
        )
        gram += both[:, :feats] + both[:, feats:]
        gram += jnp.dot(at_lo[:, cols], a_hi[m], preferred_element_type=f32)
    hi, lo = split(gram)
    gram_hi[...] = hi
    gram_lo[...] = lo

    for copy in out_loads + small_loads:
        copy.wait()

    def gram_mul(v):
        return mul(gram_hi[...], gram_lo[...], v)

    sent = []
    count = [0]

    def remote(src, dst, who):
        k = count[0]
        count[0] += 1
        copy = pltpu.make_async_remote_copy(
            src_ref=src, dst_ref=dst, send_sem=send_sem.at[k], recv_sem=recv_sem.at[k],
            device_id=who, device_id_type=MESH,
        )
        copy.start()
        sent.append(copy)
        return copy

    stores = []

    def store(src, dst):
        copy = pltpu.make_async_copy(src, dst, store_sem.at[len(stores)])
        copy.start()
        stores.append(copy)

    theta = (cheb_high + cheb_low) / 2.0
    delta = (cheb_high - cheb_low) / 2.0
    sigma = theta / delta

    for it in range(ITERS):
        last = it + 1 == ITERS
        start = v_coef[it] - v_tdual[it]
        outs = (v_tshare[...] + v_sdual[...]).reshape(rows, K)

        resid = mul(at_hi[...], at_lo[...], outs) - gram_mul(start)
        search = resid * (1.0 / theta)
        z = start + search
        rho_old = 1.0 / sigma
        for step in range(CHEB - 1):
            resid = resid - search - gram_mul(search)
            rho_new = 1.0 / (2.0 * sigma - rho_old)
            search = (rho_new * rho_old) * search + (2.0 * rho_new / delta) * resid
            rho_old = rho_new
            z = z + search
        zc[it] = z.reshape(NX, NL, B, K)
        if it == 0:
            pl.semaphore_wait(barrier, len(partners))

        to_x = [
            remote(zc.at[it, (x + p) % NX], x_in.at[it, p - 1], samp_dev((x + p) % NX, l))
            for p in x_order
        ]

        z_hi, z_lo = split(z)
        z_both = jnp.concatenate([z_hi, z_lo], axis=1)

        def forward(m):
            both = jnp.dot(a_hi[m], z_both, preferred_element_type=f32)
            got = both[:, :K] + both[:, K:] + jnp.dot(a_lo[m], z_hi, preferred_element_type=f32)
            ps[it, m] = got.reshape(NY, NH, B, K)

        forward(other)
        to_pair = {
            p: remote(
                ps.at[it, other, (y + p) % NY], pair_in.at[it, (y + p) % NY], feat_dev(h, y, other)
            )
            for p in y_order + [0]
        }
        forward(c)

        to_y = {}
        for p in y_order:
            to_pair[p].wait_recv()
            q = (y + p) % NY
            y_out[it, p] = ps[it, c, q] + pair_in[it, q]
            to_y[p] = remote(y_out.at[it, p], y_in.at[it, p - 1], feat_dev(h, q, c))
        to_pair[0].wait_recv()
        own = ps[it, c, y] + pair_in[it, y]

        for copy in to_x:
            copy.wait_recv()
        l_out[it] = zc[it, x] + x_in[it, 0] + x_in[it, 1] + x_in[it, 2] if NX == 4 else sum(
            [x_in[it, k] for k in range(NX - 1)], zc[it, x]
        )
        to_l = [
            remote(l_out.at[it, (l + p) % NL], l_in.at[it, p - 1], samp_dev(x, (l + p) % NL))
            for p in l_order
        ]

        for p in y_order:
            to_y[p].wait_recv()
            own = own + y_in[it, p - 1]
        h_out[it] = own
        to_h = [
            remote(h_out.at[it, (h + p) % NH], h_in.at[it, p - 1], feat_dev((h + p) % NH, y, c))
            for p in h_order
        ]

        value = v_coef[it] - v_cdual[it]
        half_coef = value - jnp.clip(value, -l1_weight, l1_weight)
        zc[it + ITERS] = half_coef.reshape(NX, NL, B, K)
        for copy in to_l:
            copy.wait_recv()
        mine = zc[it + ITERS, x, l] + l_out[it, l]
        for k in range(NL - 1):
            mine = mine + l_in[it, k]
        cnew[it, x, l] = mine * (1.0 / (NX * NL + 1))
        from_l = [
            remote(cnew.at[it, x, l], cnew.at[it, x, l], samp_dev(x, (l + p) % NL)) for p in l_order
        ]

        resid_t = v_share[...] - v_sdual[c, y, h] - v_targets[...]
        half_share = v_targets[...] + resid_t - jnp.clip(resid_t * 0.5, -huber_width, huber_width)
        for copy in to_h:
            copy.wait_recv()
        total = h_out[it, h]
        for k in range(NH - 1):
            total = total + h_in[it, k]
        own_excess = (half_share - total) * (1.0 / (NH * NY * NC + 1))
        exc[it, c, y, h] = own_excess
        v_share[...] = half_share - own_excess
        from_h = [
            remote(exc.at[it, c, y, h], exc.at[it, c, y, h], feat_dev((h + p) % NH, y, c))
            for p in h_order
        ]

        for copy in from_l:
            copy.wait_recv()
        from_x = [
            remote(cnew.at[it, x], cnew.at[it, x], samp_dev((x + p) % NX, l)) for p in x_order
        ]

        for copy in from_h:
            copy.wait_recv()
        from_y = {
            p: remote(exc.at[it, c, y], exc.at[it, c, y], feat_dev(h, (y + p) % NY, c))
            for p in y_order
        }
        from_pair = [remote(exc.at[it, c, y], exc.at[it, c, y], feat_dev(h, y, other))]

        for copy in from_x:
            copy.wait_recv()
        coef_new = cnew[it].reshape(feats, K)
        v_coef[it + 1] = coef_new
        v_cdual[it + 1] = v_cdual[it] + half_coef - coef_new
        v_tdual[it + 1] = v_tdual[it] + zc[it].reshape(feats, K) - coef_new
        if last:
            store(v_coef.at[it + 1], o_coef)
            store(v_cdual.at[it + 1], o_cdual)
            store(v_tdual.at[it + 1], o_tdual)
            store(v_share, o_share)

        for p in reversed(y_order):
            from_y[p].wait_recv()
            q = (y - p + NY) % NY
            from_pair.append(
                remote(exc.at[it, c, q], exc.at[it, c, q], feat_dev(h, y, other))
            )
        for copy in from_pair:
            copy.wait_recv()
        v_sdual[...] = v_sdual[...] + exc[it]
        v_tshare[...] = ps[it] + exc[it]
        if last:
            for src, dst in ((v_sdual, o_sdual), (v_tshare, o_tshare)):
                for m in range(NC):
                    for k in range(NH):
                        store(src.at[m, :, k], dst.at[k, :, m])

    for copy in sent:
        copy.wait_send()
    for copy in stores:
        copy.wait()


def shards(data, targets, coef, cdual, tdual, share, sdual, tshare):
    feats = NX * NL * B
    whole = (NH, NY, NC, B)
    perm = (NC, NY, NH, B)
    half = NY * NH * B
    hbm = pl.BlockSpec(memory_space=pltpu.HBM)
    copies = ITERS * (2 * NC * (NY - 1) + 2 * (NH + NX + NL - 3) + (NC - 1) * 2 * NY - (NC - 1) * 0)
    vm = pltpu.VMEM
    outs = pl.pallas_call(
        body,
        out_shape=[
            jax.ShapeDtypeStruct((feats, K), f32),
            jax.ShapeDtypeStruct((feats, K), f32),
            jax.ShapeDtypeStruct((feats, K), f32),
            jax.ShapeDtypeStruct((B, K), f32),
            jax.ShapeDtypeStruct(whole + (K,), f32),
            jax.ShapeDtypeStruct(whole + (K,), f32),
        ],
        in_specs=[hbm] * 8,
        out_specs=[hbm] * 6,
        scratch_shapes=[
            vm(perm + (feats,), f32),
            vm((NC, half, feats), bf16),
            vm((NC, half, feats), bf16),
            vm((feats, NC * half), bf16),
            vm((feats, NC * half), bf16),
            vm((feats, feats), bf16),
            vm((feats, feats), bf16),
            vm((B, K), f32),
            vm((ITERS + 1, feats, K), f32),
            vm((ITERS + 1, feats, K), f32),
            vm((ITERS + 1, feats, K), f32),
            vm((B, K), f32),
            vm(perm + (K,), f32),
            vm(perm + (K,), f32),
            vm((ITERS,) + perm + (K,), f32),
            vm((ITERS, NY, NH, B, K), f32),
            vm((ITERS, NY, NH, B, K), f32),
            vm((ITERS, NY - 1, NH, B, K), f32),
            vm((ITERS, NH, B, K), f32),
            vm((ITERS, NH - 1, B, K), f32),
            vm((ITERS,) + perm + (K,), f32),
            vm((2 * ITERS, NX, NL, B, K), f32),
            vm((ITERS, NX - 1, NL, B, K), f32),
            vm((ITERS, NL, B, K), f32),
            vm((ITERS, NL - 1, B, K), f32),
            vm((ITERS, NX, NL, B, K), f32),
            pltpu.SemaphoreType.DMA((3 * NC * NH + 5,)),
            pltpu.SemaphoreType.DMA((2 * NC * NH + 4,)),
            pltpu.SemaphoreType.DMA((copies,)),
            pltpu.SemaphoreType.DMA((copies,)),
        ],
        compiler_params=pltpu.CompilerParams(
            collective_id=0, has_side_effects=True, vmem_limit_bytes=48 * 1024 * 1024
        ),
    )(
        data.reshape(whole + (feats,)), targets, coef, cdual, tdual[0], share,
        sdual.reshape(whole + (K,)), tshare.reshape(whole + (K,)),
    )
    coef, cdual, tdual, share, sdual, tshare = outs
    rows = NC * half
    return (coef, cdual, tdual[None], share, sdual.reshape(rows, K), tshare.reshape(1, rows, K))


def solution(mesh):
    return jax.shard_map(
        shards,
        mesh=mesh,
        in_specs=(
            P("samp", "feat"),
            P(("samp", "feat"), None),
            P("feat", None),
            P("feat", None),
            P("samp", "feat", None),
            P(("samp", "feat"), None),
            P("samp", None),
            P("feat", "samp", None),
        ),
        out_specs=(
            P("feat", None),
            P("feat", None),
            P("samp", "feat", None),
            P(("samp", "feat"), None),
            P("samp", None),
            P("feat", "samp", None),
        ),
        check_vma=False,
    )
```

time: 1750 us -> 101 us (0.06)
  waiting for transfers between devices: 1470 us -> 0 us
  blocking collectives: 217 us -> 0 us
  Pallas kernels: 0 us -> 88.4 us
  matrix products: 26.1 us -> 0 us
    psum x4 -> x0, waiting for transfers between devices: 1470 us -> none  [the longest x2 1360 us: shards(): whole_sum = lax.psum(proj_share, 'feat')]
    all_gather x2 -> x0, blocking collectives: 217 us -> none  [shards(): half_all = lax.all_gather(half_share, 'feat', axis=0, tiled=True)]
    pallas_call x0 -> x1, Pallas kernels: none -> 88.4 us  [shards(): pl.pallas_call(body, out_shape=[jax.ShapeDtypeStruct((feats, K), f32), ja...]
    dot_general x24 -> x0, matrix products: 26.1 us -> none  [the longest x12 16.3 us: forward_mul(): return jnp.dot(data, vector, precision=high)]
  transfers between devices with their start and end apart: 4 -> 0, of which waited for: 4 -> 0; matrix products, arithmetic and copies ran while one was open for 1% -> 0% of each run, Pallas kernels for 0% -> 0%
where the time goes in v1:
time: 101 us
  Pallas kernels  88.4 us (88%)
  local copies, waits for them, and re-layouts  11.6 us (11%)
    pallas_call x1, Pallas kernels, shards(): pl.pallas_call(body, out_shape=[jax.ShapeDtypeStruct((feats, K), f32), ja...  88.4 us
    unnamed x22, local copies, waits for them, and re-layouts  11.6 us

profile of v1, /device:TPU:1, one launch (start us, length us, event | category | flops | bytes accessed | tf_op | source)
XLA Modules:
  0.0 100.6 jit_solution(276146959921495456)
XLA Ops:
  0.6 0.0 copy-start
  0.6 1.2 %copy-done = f32[1024,256]{1,0:T(8,128)S(1)} copy-done((f32[1024,256]{1,0:T(8,128)S(1)}, f32[1024,256]{1,0:T(8,128)}, u32[]{:S(2)}) %copy-start) | copy-done | bytes 1048600
  1.9 0.0 copy-start.1
  1.9 1.0 %copy-done.1 = f32[1024,128]{1,0:T(8,128)S(1)} copy-done((f32[1024,128]{1,0:T(8,128)S(1)}, f32[1024,128]{1,0:T(8,128)}, u32[]{:S(2)}) %copy-start.1) | copy-done | bytes 524312
  2.9 0.0 copy-start.2
  2.9 1.0 %copy-done.2 = f32[1,1024,128]{2,1,0:T(8,128)S(1)} copy-done((f32[1,1024,128]{2,1,0:T(8,128)S(1)}, f32[1,1024,128]{2,1,0:T(8,128)}, u32[]{:S(2)}) %copy-start.2) | copy-done | bytes 524312
  3.9 0.0 copy-start.3
  3.9 0.9 copy-done.3
  4.8 0.0 copy-start.4
  4.9 0.9 copy-done.4
  5.8 0.0 copy-start.5
  5.8 0.9 copy-done.5
  6.7 0.0 copy-start.6
  6.7 0.7 copy-done.6
  7.4 0.0 copy-start.7
  7.4 0.7 copy-done.7
  8.1 88.4 %shard_map.127 = (f32[256,128]{1,0:T(8,128)S(1)}, f32[256,128]{1,0:T(8,128)S(1)}, f32[256,128]{1,0:T(8,128)S(1)}, f32[16,128]{1,0:T(8,128)S(1)}, f32[4,8,2,16,12...) custom-call(f32[4,8,2,16,256]{4,3,2,1,0:T(8,128)S(1)} %bitcast.7, f32[16,128]{1,0:T(8,128)S(1)} %copy-done.6, ...), custom_call_target="tpu_custom_call" | custom-call | tf_op jit(solution)/shard_map/pallas_call | solution.py:305
  96.5 0.7 copy.20
  97.1 0.7 copy.21
  97.8 0.7 copy.22
  98.5 0.6 copy.23
  99.1 0.8 copy.24
  99.8 0.8 copy.25
Async XLA Ops:
  0.6 1.2 %copy-start = (f32[1024,256]{1,0:T(8,128)S(1)}, f32[1024,256]{1,0:T(8,128)}, u32[]{:S(2)}) copy-start(f32[1024,256]{1,0:T(8,128)} %param.8) | copy-start | bytes 3145732
  1.9 1.0 %copy-start.1 = (f32[1024,128]{1,0:T(8,128)S(1)}, f32[1024,128]{1,0:T(8,128)}, u32[]{:S(2)}) copy-start(f32[1024,128]{1,0:T(8,128)} %param.14) | copy-start | bytes 1572868
  2.9 1.0 %copy-start.2 = (f32[1,1024,128]{2,1,0:T(8,128)S(1)}, f32[1,1024,128]{2,1,0:T(8,128)}, u32[]{:S(2)}) copy-start(f32[1,1024,128]{2,1,0:T(8,128)} %param.15) | copy-start | bytes 1572868
  3.9 0.9 copy-start.3
  4.8 0.9 copy-start.4
  5.8 0.9 copy-start.5
  6.7 0.7 copy-start.6
  7.4 0.7 copy-start.7

commit v2 on v1

v2 whole, which is shorter than its diff:
```python
import functools

import jax
import jax.numpy as jnp
from jax import lax
from jax.experimental import pallas as pl
from jax.experimental.pallas import tpu as pltpu
from jax.sharding import PartitionSpec as P

ITERS = 2
CHEB = 5

cheb_low = 1.0
cheb_high = 3.2
l1_weight = 0.2
huber_width = 4.0

NX, NL, NH, NY, NC = 4, 4, 4, 8, 2
B = 16
K = 128
NG = 2
VMEM_MIB = 60

MESH = pl.DeviceIdType.MESH
f32 = jnp.float32
bf16 = jnp.bfloat16


def split(v):
    hi = v.astype(bf16)
    return hi, (v - hi.astype(f32)).astype(bf16)


def mul2(lhs_hi, lhs_lo, hi, lo):
    n = hi.shape[1]
    both = jnp.dot(lhs_hi, jnp.concatenate([hi, lo], axis=1), preferred_element_type=f32)
    return both[:, :n] + both[:, n:] + jnp.dot(lhs_lo, hi, preferred_element_type=f32)


def mul(lhs_hi, lhs_lo, v):
    return mul2(lhs_hi, lhs_lo, *split(v))


def far_first(n):
    return sorted(range(1, n), key=lambda p: -min(p, n - p))


def body(
    data, targets, coef, cdual, tdual, share, sdual, tshare,
    o_coef, o_cdual, o_tdual, o_share, o_sdual, o_tshare,
    a32, a_hi, a_lo, at_hi, at_lo, w_hi, w_lo, gram_hi, gram_lo, q_hi, q_lo,
    v_st, v_coef, v_cdual, v_tdual, v_sdual, v_tshare,
    ps, pair_in, y_out, y_in, h_all, exc, zc, half_c, x_in, l_all, cnew,
    load_sem, send_sem, recv_sem,
):
    half = NY * NH * B
    rows = NC * half
    feats = NX * NL * B
    s, f = lax.axis_index("samp"), lax.axis_index("feat")
    x, l = s // NL, s % NL
    h, y, c = f // (NY * NC), (f // NC) % NY, f % NC
    other = 1 - c

    def feat_dev(h_, y_, c_):
        return (s, (h_ * NY + y_) * NC + c_)

    def samp_dev(x_, l_):
        return (x_ * NL + l_, f)

    y_order, h_order, x_order, l_order = far_first(NY), far_first(NH), far_first(NX), far_first(NL)
    groups = [slice(g * (NH // NG), (g + 1) * (NH // NG)) for g in range(NG)]

    barrier = pltpu.get_barrier_semaphore()
    partners = (
        [feat_dev((h + p) % NH, y, c) for p in h_order]
        + [feat_dev(h, (y + p) % NY, c) for p in y_order]
        + [samp_dev((x + p) % NX, l) for p in x_order]
        + [samp_dev(x, (l + p) % NL) for p in l_order]
        + [feat_dev(h, y, other)]
    )
    for who in partners:
        pl.semaphore_signal(barrier, inc=1, device_id=who, device_id_type=MESH)

    loads = []

    def load(src, dst):
        copy = pltpu.make_async_copy(src, dst, load_sem.at[len(loads)])
        copy.start()
        loads.append(copy)
        return copy

    data_loads = [load(data.at[k, :, m], a32.at[m, :, k]) for m in range(NC) for k in range(NH)]
    out_loads = [
        load(src.at[k, :, m], dst.at[m, :, k])
        for src, dst in ((tshare, v_tshare), (sdual, v_sdual))
        for m in range(NC)
        for k in range(NH)
    ]
    small_loads = [
        load(coef, v_coef.at[0]),
        load(tdual, v_tdual.at[0]),
        load(cdual, v_cdual.at[0]),
        load(share, v_st.at[0, h]),
        load(targets, v_st.at[1, h]),
    ]

    for copy in data_loads:
        copy.wait()
    gram = jnp.zeros((feats, feats), f32)
    for m in range(NC):
        a = a32[m].reshape(half, feats)
        hi, lo = split(a)
        a_hi[m] = hi
        a_lo[m] = lo
        t_hi, t_lo = split(a.T)
        at_hi[m] = t_hi
        at_lo[m] = t_lo
        gram += mul2(t_hi, t_lo, hi, lo)
    hi, lo = split(gram)
    gram_hi[...] = hi
    gram_lo[...] = lo

    for copy in out_loads + small_loads:
        copy.wait()

    def gram_mul(v):
        return mul(gram_hi[...], gram_lo[...], v)

    sent = []
    count = [0]

    def remote(src, dst, who):
        k = count[0]
        count[0] += 1
        copy = pltpu.make_async_remote_copy(
            src_ref=src, dst_ref=dst, send_sem=send_sem.at[k], recv_sem=recv_sem.at[k],
            device_id=who, device_id_type=MESH,
        )
        copy.start()
        sent.append(copy)
        return copy

    theta = (cheb_high + cheb_low) / 2.0
    delta = (cheb_high - cheb_low) / 2.0
    sigma = theta / delta

    def chebyshev(resid):
        search = resid * (1.0 / theta)
        z = search
        rho_old = 1.0 / sigma
        for step in range(CHEB - 1):
            resid = resid - search - gram_mul(search)
            rho_new = 1.0 / (2.0 * sigma - rho_old)
            search = (rho_new * rho_old) * search + (2.0 * rho_new / delta) * resid
            rho_old = rho_new
            z = z + search
        return z

    for it in range(ITERS):
        last = it + 1 == ITERS
        if it == 0:
            start = v_coef[0] - v_tdual[0]
            resid = -gram_mul(start)
            for m in range(NC):
                resid += mul(at_hi[m], at_lo[m], (v_tshare[m] + v_sdual[m]).reshape(half, K))
            z = start + chebyshev(resid)
            pl.semaphore_wait(barrier, len(partners))
        zc[it] = z.reshape(NX, NL, B, K)

        to_x = [
            remote(zc.at[it, (x + p) % NX], x_in.at[it, p - 1], samp_dev((x + p) % NX, l))
            for p in x_order
        ]

        z_hi, z_lo = split(z)

        def forward(m):
            ps[it, m] = mul2(a_hi[m], a_lo[m], z_hi, z_lo).reshape(NY, NH, B, K)

        forward(other)
        to_pair = {
            p: remote(
                ps.at[it, other, (y + p) % NY], pair_in.at[it, (y + p) % NY], feat_dev(h, y, other)
            )
            for p in y_order + [0]
        }
        forward(c)
        if it == 0:
            st = [
                remote(v_st.at[:, h], v_st.at[:, h], feat_dev((h + p) % NH, y, c)) for p in h_order
            ]

        to_y = {}
        for g, part in enumerate(groups):
            for p in y_order:
                if g == 0:
                    to_pair[p].wait_recv()
                q = (y + p) % NY
                y_out[it, p, part] = ps[it, c, q, part] + pair_in[it, q, part]
                to_y[g, p] = remote(
                    y_out.at[it, p, part], y_in.at[it, p - 1, part], feat_dev(h, q, c)
                )
        to_pair[0].wait_recv()
        own = ps[it, c, y] + pair_in[it, y]

        summed = zc[it, x]
        for p, copy in zip(x_order, to_x, strict=True):
            copy.wait_recv()
            summed = summed + x_in[it, p - 1]
        l_all[it, l] = summed
        to_l = [
            remote(l_all.at[it, l], l_all.at[it, l], samp_dev(x, (l + p) % NL)) for p in l_order
        ]

        to_h = {}
        for g, part in enumerate(groups):
            total = own[part]
            for p in reversed(y_order):
                to_y[g, p].wait_recv()
                total = total + y_in[it, p - 1, part]
            h_all[it, g, h] = total
            to_h[g] = [
                remote(h_all.at[it, g, h], h_all.at[it, g, h], feat_dev((h + p) % NH, y, c))
                for p in h_order
            ]

        value = v_coef[it] - v_cdual[it]
        half_c[it] = (value - jnp.clip(value, -l1_weight, l1_weight)).reshape(NX, NL, B, K)
        for copy in to_l:
            copy.wait_recv()
        summed = l_all[it, 0]
        for k in range(1, NL):
            summed = summed + l_all[it, k]
        cnew[it, x] = (half_c[it, x] + summed) * (1.0 / (NX * NL + 1))
        from_x = [
            remote(cnew.at[it, x], cnew.at[it, x], samp_dev((x + p) % NX, l)) for p in x_order
        ]

        if it == 0:
            eye = (
                lax.broadcasted_iota(jnp.int32, (feats, feats), 0)
                == lax.broadcasted_iota(jnp.int32, (feats, feats), 1)
            ).astype(f32)
            hi, lo = split(chebyshev(eye))
            q_hi[...] = hi
            q_lo[...] = lo
            for m in range(NC):
                w = mul2(hi, lo, at_hi[m], at_lo[m])
                hi_w, lo_w = split(w)
                w_hi[m] = hi_w
                w_lo[m] = lo_w
        if not last:
            base = jnp.zeros((feats, K), f32)
            for m in range(NC):
                base += mul(w_hi[m], w_lo[m], (ps[it, m] + v_sdual[m]).reshape(half, K))

        if it == 0:
            for copy in st:
                copy.wait()
            sent[:] = [copy for copy in sent if not any(copy is k for k in st)]
        from_y, from_pair = {}, []
        for g, part in enumerate(groups):
            old, goal = v_st[0, part], v_st[1, part]
            resid_t = old - v_sdual[c, y, part] - goal
            half_share = goal + resid_t - jnp.clip(resid_t * 0.5, -huber_width, huber_width)
            for copy in to_h[g]:
                copy.wait_recv()
            total = h_all[it, g, 0]
            for k in range(1, NH):
                total = total + h_all[it, g, k]
            excess = (half_share - total) * (1.0 / (NH * NY * NC + 1))
            exc[it, c, y, part] = excess
            here = exc.at[it, c, y, part]
            for p in y_order:
                from_y[g, p] = remote(here, here, feat_dev(h, (y + p) % NY, c))
            from_pair.append(remote(here, here, feat_dev(h, y, other)))
            share_new = half_share - excess
            if last:
                v_st[1, part] = share_new
            else:
                v_st[2, part] = share_new

        for copy in from_x:
            copy.wait_recv()
        coef_new = cnew[it].reshape(feats, K)
        cdual_new = v_cdual[it] + half_c[it].reshape(feats, K) - coef_new
        tdual_new = v_tdual[it] + zc[it].reshape(feats, K) - coef_new
        if last:
            o_coef[...] = coef_new
            o_cdual[...] = cdual_new
            o_tdual[...] = tdual_new
            o_share[...] = v_st[1, h]
        else:
            v_coef[it + 1] = coef_new
            v_cdual[it + 1] = cdual_new
            v_tdual[it + 1] = tdual_new
            start = coef_new - tdual_new
            base = base + start - mul(q_hi[...], q_lo[...], gram_mul(start))

        for g, part in enumerate(groups):
            for p in reversed(y_order):
                from_y[g, p].wait_recv()
                q = (y - p + NY) % NY
                there = exc.at[it, c, q, part]
                from_pair.append(remote(there, there, feat_dev(h, y, other)))
        z = None if last else base

        for m in (c, other):
            if m is other:
                for copy in from_pair:
                    copy.wait_recv()
            got = exc[it, m]
            if last:
                o_sdual[m] = v_sdual[m] + got
                o_tshare[m] = ps[it, m] + got
            else:
                z = z + mul(w_hi[m], w_lo[m], (got + got).reshape(half, K))
        if not last:
            v_sdual[...] = v_sdual[...] + exc[it]
            v_st[0] = v_st[2]

    for copy in sent:
        copy.wait_send()


def hand_over(*refs):
    n = (len(refs) - 1) // 2
    sem = refs[-1]
    copies = []

    def start(src, dst):
        copies.append(pltpu.make_async_copy(src, dst, sem.at[len(copies)]))
        copies[-1].start()

    for src, dst in zip(refs[:n], refs[n:-1], strict=True):
        if len(src.shape) == 2:
            start(src, dst)
        else:
            for m in range(NC):
                for k in range(NH):
                    start(src.at[m, :, k], dst.at[k, :, m])
    for copy in copies:
        copy.wait()


def shards(data, targets, coef, cdual, tdual, share, sdual, tshare):
    feats = NX * NL * B
    whole = (NH, NY, NC, B)
    perm = (NC, NY, NH, B)
    half = NY * NH * B
    rows = NC * half
    hbm = pl.BlockSpec(memory_space=pltpu.HBM)
    vmem = pl.BlockSpec(memory_space=pltpu.VMEM)
    vm = pltpu.VMEM
    a_sweep = 2 * NG * (NY - 1) + NG * (NH - 1) + 2 * (NX - 1) + (NL - 1) + NY + NG * NY
    copies = ITERS * a_sweep + NH - 1
    shapes = [(feats, K)] * 3 + [(B, K)]
    outs = pl.pallas_call(
        body,
        out_shape=[jax.ShapeDtypeStruct(k, f32) for k in shapes + [perm + (K,)] * 2],
        in_specs=[hbm] * 8,
        out_specs=[vmem] * 6,
        scratch_shapes=[
            vm(perm + (feats,), f32),
            vm((NC, half, feats), bf16),
            vm((NC, half, feats), bf16),
            vm((NC, feats, half), bf16),
            vm((NC, feats, half), bf16),
            vm((NC, feats, half), bf16),
            vm((NC, feats, half), bf16),
            vm((feats, feats), bf16),
            vm((feats, feats), bf16),
            vm((feats, feats), bf16),
            vm((feats, feats), bf16),
            vm((3, NH, B, K), f32),
            vm((ITERS, feats, K), f32),
            vm((ITERS, feats, K), f32),
            vm((ITERS, feats, K), f32),
            vm(perm + (K,), f32),
            vm(perm + (K,), f32),
            vm((ITERS,) + perm + (K,), f32),
            vm((ITERS, NY, NH, B, K), f32),
            vm((ITERS, NY, NH, B, K), f32),
            vm((ITERS, NY - 1, NH, B, K), f32),
            vm((ITERS, NG, NH, NH // NG, B, K), f32),
            vm((ITERS,) + perm + (K,), f32),
            vm((ITERS, NX, NL, B, K), f32),
            vm((ITERS, NX, NL, B, K), f32),
            vm((ITERS, NX - 1, NL, B, K), f32),
            vm((ITERS, NL, NL, B, K), f32),
            vm((ITERS, NX, NL, B, K), f32),
            pltpu.SemaphoreType.DMA((3 * NC * NH + 5,)),
            pltpu.SemaphoreType.DMA((copies,)),
            pltpu.SemaphoreType.DMA((copies,)),
        ],
        compiler_params=pltpu.CompilerParams(
            collective_id=0, has_side_effects=True, vmem_limit_bytes=VMEM_MIB * 1024 * 1024
        ),
    )(
        data.reshape(whole + (feats,)), targets, coef, cdual, tdual[0], share,
        sdual.reshape(whole + (K,)), tshare.reshape(whole + (K,)),
    )
    coef, cdual, tdual, share, sdual, tshare = pl.pallas_call(
        hand_over,
        out_shape=[jax.ShapeDtypeStruct(k, f32) for k in shapes + [whole + (K,)] * 2],
        in_specs=[vmem] * 6,
        out_specs=[hbm] * 6,
        scratch_shapes=[pltpu.SemaphoreType.DMA((4 + 2 * NC * NH,))],
    )(*outs)
    return (coef, cdual, tdual[None], share, sdual.reshape(rows, K), tshare.reshape(1, rows, K))


def solution(mesh):
    return jax.shard_map(
        shards,
        mesh=mesh,
        in_specs=(
            P("samp", "feat"),
            P(("samp", "feat"), None),
            P("feat", None),
            P("feat", None),
            P("samp", "feat", None),
            P(("samp", "feat"), None),
            P("samp", None),
            P("feat", "samp", None),
        ),
        out_specs=(
            P("feat", None),
            P("feat", None),
            P("samp", "feat", None),
            P(("samp", "feat"), None),
            P("samp", None),
            P("feat", "samp", None),
        ),
        check_vma=False,
    )
```

time: 101 us -> 77.7 us (0.77)
  Pallas kernels: 88.4 us -> 76.3 us
  local copies, waits for them, and re-layouts: 11.6 us -> 0 us
    pallas_call x1 -> x2, Pallas kernels: 88.4 us -> 76.3 us  [the longest x1 73.6 us: shards(): pl.pallas_call(body, out_shape=[jax.ShapeDtypeStruct(k, f32) for k in sha...]
    unnamed x22 -> x0, local copies, waits for them, and re-layouts: 11.6 us -> none
where the time goes in v2:
time: 77.7 us; the launch traced here: 76.9 us
  Pallas kernels  76.3 us (98%)
    pallas_call x1, Pallas kernels, shards(): pl.pallas_call(body, out_shape=[jax.ShapeDtypeStruct(k, f32) for k in sha...  73.6 us
    pallas_call x1, Pallas kernels, shards(): pl.pallas_call(hand_over, out_shape=[jax.ShapeDtypeStruct(k, f32) for k i...  2.68 us

profile of v2, /device:TPU:1, one launch (start us, length us, event | category | flops | bytes accessed | tf_op | source)
XLA Modules:
  0.0 76.9 jit_solution(16051958977222151743)
XLA Ops:
  0.6 73.6 %shard_map.127 = (f32[256,128]{1,0:T(8,128)}, f32[256,128]{1,0:T(8,128)}, f32[256,128]{1,0:T(8,128)}, f32[16,128]{1,0:T(8,128)}, f32[2,8,4,16,128]{4,3,2,1,0:T(8,128)}, /*index=5*/f32[2,8,4,16,128]{4,3,2,1,0:T(8,128)}) custom-call(f32[4,8,2,16,256]{4,3,2,1,0:T(8,128)} %bitcast.7, f32[16,128]{1,0:T(8,128)} %targets.1, f32[256,128]{1,0:T(8,128)} %coef.1, ...), custom_call_target="tpu_custom_call" | custom-call | tf_op jit(solution)/shard_map/pallas_call | solution.py:358
  74.2 2.7 %shard_map.128 = (f32[256,128]{1,0:T(8,128)}, f32[256,128]{1,0:T(8,128)}, f32[256,128]{1,0:T(8,128)}, f32[16,128]{1,0:T(8,128)}, f32[4,8,2,16,128]{4,3,2,1,0:T(8,128)}, /*index=5*/f32[4,8,2,16,128]{4,3,2,1,0:T(8,128)}) custom-call(f32[256,128]{1,0:T(8,128)} %get-tuple-element.18.refs_0_, f32[256,128]{1,0:T(8,128)} %get-tuple-element.19.refs_1_, ...), custom_call_target="tpu_custom_call" | custom-call | tf_op jit(solution)/shard_map/pallas_call | solution.py:403

commit v3 on v2

--- a/solution.py
+++ b/solution.py
@@ -357,7 +357,7 @@
     shapes = [(feats, K)] * 3 + [(B, K)]
     outs = pl.pallas_call(
         body,
-        out_shape=[jax.ShapeDtypeStruct(k, f32) for k in shapes + [perm + (K,)] * 2],
+        out_shape=[pltpu.VMEM(k, f32) for k in shapes + [perm + (K,)] * 2],
         in_specs=[hbm] * 8,
         out_specs=[vmem] * 6,
         scratch_shapes=[
@@ -406,6 +406,7 @@
         in_specs=[vmem] * 6,
         out_specs=[hbm] * 6,
         scratch_shapes=[pltpu.SemaphoreType.DMA((4 + 2 * NC * NH,))],
+        compiler_params=pltpu.CompilerParams(vmem_limit_bytes=4 * 1024 * 1024),
     )(*outs)
     return (coef, cdual, tdual[None], share, sdual.reshape(rows, K), tshare.reshape(1, rows, K))
 

time: 77.7 us -> 75.6 us (0.973)
  Pallas kernels: 76.3 us -> 73.7 us
    pallas_call x1, Pallas kernels: 2.68 us -> 1.26 us  [shards(): pl.pallas_call(hand_over, out_shape=[jax.ShapeDtypeStruct(k, f32) for k i...]
    pallas_call x1, Pallas kernels: 73.6 us -> 72.4 us  [shards(): pl.pallas_call(body, out_shape=[pltpu.VMEM(k, f32) for k in shapes + [per...]
where the time goes in v3:
time: 75.6 us; the launch traced here: 74.3 us
  Pallas kernels  73.7 us (97%)
    pallas_call x1, Pallas kernels, shards(): pl.pallas_call(body, out_shape=[pltpu.VMEM(k, f32) for k in shapes + [per...  72.4 us

profile of v3, /device:TPU:1, one launch (start us, length us, event | category | flops | bytes accessed | tf_op | source)
XLA Modules:
  0.0 74.3 jit_solution(4224425780515114476)
XLA Ops:
  0.6 72.4 %shard_map.127 = (f32[256,128]{1,0:T(8,128)S(1)}, f32[256,128]{1,0:T(8,128)S(1)}, f32[256,128]{1,0:T(8,128)S(1)}, f32[16,128]{1,0:T(8,128)S(1)}, f32[2,8,4,16,12...) custom-call(f32[4,8,2,16,256]{4,3,2,1,0:T(8,128)} %bitcast.7, f32[16,128]{1,0:T(8,128)} %targets.1, ...), custom_call_target="tpu_custom_call" | custom-call | tf_op jit(solution)/shard_map/pallas_call | solution.py:358
  73.1 1.3 %shard_map.128 = (f32[256,128]{1,0:T(8,128)}, f32[256,128]{1,0:T(8,128)}, f32[256,128]{1,0:T(8,128)}, f32[16,128]{1,0:T(8,128)}, f32[4,8,2,16,128]{4,3,2,1,0:T(8,128)}, /*index=5*/f32[4,8,2,16,128]{4,3,2,1,0:T(8,128)}) custom-call(f32[256,128]{1,0:T(8,128)S(1)} %get-tuple-element.18.refs_0_, f32[256,128]{1,0:T(8,128)S(1)} %get-tuple-element.19.refs_1_, ...), custom_call_target="tpu_custom_call" | custom-call | tf_op jit(solution)/shard_map/pallas_call | solution.py:403

commit v4 on v3

--- a/solution.py
+++ b/solution.py
@@ -41,6 +41,27 @@
     return mul2(lhs_hi, lhs_lo, *split(v))
 
 
+def step_polynomial():
+    theta = (cheb_high + cheb_low) / 2.0
+    delta = (cheb_high - cheb_low) / 2.0
+    sigma = theta / delta
+    resid = [1.0] + [0.0] * (CHEB - 1)
+    search = [k / theta for k in resid]
+    z = list(search)
+    rho_old = 1.0 / sigma
+    for _ in range(CHEB - 1):
+        moved = [0.0] + search[:-1]
+        resid = [r - d - m for r, d, m in zip(resid, search, moved, strict=True)]
+        rho_new = 1.0 / (2.0 * sigma - rho_old)
+        search = [
+            rho_new * rho_old * d + (2.0 * rho_new / delta) * r
+            for d, r in zip(search, resid, strict=True)
+        ]
+        rho_old = rho_new
+        z = [k + d for k, d in zip(z, search, strict=True)]
+    return z
+
+
 def far_first(n):
     return sorted(range(1, n), key=lambda p: -min(p, n - p))
 
@@ -48,7 +69,7 @@
 def body(
     data, targets, coef, cdual, tdual, share, sdual, tshare,
     o_coef, o_cdual, o_tdual, o_share, o_sdual, o_tshare,
-    a32, a_hi, a_lo, at_hi, at_lo, w_hi, w_lo, gram_hi, gram_lo, q_hi, q_lo,
+    a32, a_hi, a_lo, at_hi, at_lo, w_hi, w_lo, gram_hi, gram_lo, powers, q_hi, q_lo,
     v_st, v_coef, v_cdual, v_tdual, v_sdual, v_tshare,
     ps, pair_in, y_out, y_in, h_all, exc, zc, half_c, x_in, l_all, cnew,
     load_sem, send_sem, recv_sem,
@@ -104,10 +125,10 @@
         load(targets, v_st.at[1, h]),
     ]
 
-    for copy in data_loads:
-        copy.wait()
     gram = jnp.zeros((feats, feats), f32)
     for m in range(NC):
+        for copy in data_loads[m * NH : (m + 1) * NH]:
+            copy.wait()
         a = a32[m].reshape(half, feats)
         hi, lo = split(a)
         a_hi[m] = hi
@@ -117,14 +138,20 @@
         at_lo[m] = t_lo
         gram += mul2(t_hi, t_lo, hi, lo)
     hi, lo = split(gram)
-    gram_hi[...] = hi
-    gram_lo[...] = lo
+    gram_hi[:feats] = hi
+    gram_lo[:feats] = lo
+    square = mul2(hi, lo, hi, lo)
+    powers[0] = gram
+    powers[1] = square
+    hi, lo = split(square)
+    gram_hi[feats:] = hi
+    gram_lo[feats:] = lo
 
     for copy in out_loads + small_loads:
         copy.wait()
 
     def gram_mul(v):
-        return mul(gram_hi[...], gram_lo[...], v)
+        return mul(gram_hi[:feats], gram_lo[:feats], v)
 
     sent = []
     count = [0]
@@ -140,21 +167,13 @@
         sent.append(copy)
         return copy
 
-    theta = (cheb_high + cheb_low) / 2.0
-    delta = (cheb_high - cheb_low) / 2.0
-    sigma = theta / delta
+    e = step_polynomial()
 
     def chebyshev(resid):
-        search = resid * (1.0 / theta)
-        z = search
-        rho_old = 1.0 / sigma
-        for step in range(CHEB - 1):
-            resid = resid - search - gram_mul(search)
-            rho_new = 1.0 / (2.0 * sigma - rho_old)
-            search = (rho_new * rho_old) * search + (2.0 * rho_new / delta) * resid
-            rho_old = rho_new
-            z = z + search
-        return z
+        both = mul(gram_hi[...], gram_lo[...], resid)
+        one, two = both[:feats], both[feats:]
+        inner = e[2] * resid + e[3] * one + e[4] * two
+        return e[0] * resid + e[1] * one + mul(gram_hi[feats:], gram_lo[feats:], inner)
 
     for it in range(ITERS):
         last = it + 1 == ITERS
@@ -241,7 +260,9 @@
                 lax.broadcasted_iota(jnp.int32, (feats, feats), 0)
                 == lax.broadcasted_iota(jnp.int32, (feats, feats), 1)
             ).astype(f32)
-            hi, lo = split(chebyshev(eye))
+            inner = e[2] * eye + e[3] * powers[0] + e[4] * powers[1]
+            outer = e[0] * eye + e[1] * powers[0]
+            hi, lo = split(outer + mul(gram_hi[feats:], gram_lo[feats:], inner))
             q_hi[...] = hi
             q_lo[...] = lo
             for m in range(NC):
@@ -368,8 +389,9 @@
             vm((NC, feats, half), bf16),
             vm((NC, feats, half), bf16),
             vm((NC, feats, half), bf16),
-            vm((feats, feats), bf16),
-            vm((feats, feats), bf16),
+            vm((2 * feats, feats), bf16),
+            vm((2 * feats, feats), bf16),
+            vm((2, feats, feats), f32),
             vm((feats, feats), bf16),
             vm((feats, feats), bf16),
             vm((3, NH, B, K), f32),

time: 75.6 us -> 75.8 us (level)
  no operation moved by 1% of the time
where the time goes in v4:
time: 75.8 us; the launch traced here: 74.6 us
  Pallas kernels  74 us (98%)
    pallas_call x1, Pallas kernels, shards(): pl.pallas_call(body, out_shape=[pltpu.VMEM(k, f32) for k in shapes + [per...  72.7 us

profile of v4, /device:TPU:1, one launch (start us, length us, event | category | flops | bytes accessed | tf_op | source)
XLA Modules:
  0.0 74.6 jit_solution(11307877020051241409)
XLA Ops:
  0.6 72.7 %shard_map.127 = (f32[256,128]{1,0:T(8,128)S(1)}, f32[256,128]{1,0:T(8,128)S(1)}, f32[256,128]{1,0:T(8,128)S(1)}, f32[16,128]{1,0:T(8,128)S(1)}, f32[2,8,4,16,12...) custom-call(f32[4,8,2,16,256]{4,3,2,1,0:T(8,128)} %bitcast.7, f32[16,128]{1,0:T(8,128)} %targets.1, ...), custom_call_target="tpu_custom_call" | custom-call | tf_op jit(solution)/shard_map/pallas_call | solution.py:379
  73.3 1.3 %shard_map.128 = (f32[256,128]{1,0:T(8,128)}, f32[256,128]{1,0:T(8,128)}, f32[256,128]{1,0:T(8,128)}, f32[16,128]{1,0:T(8,128)}, f32[4,8,2,16,128]{4,3,2,1,0:T(8,128)}, /*index=5*/f32[4,8,2,16,128]{4,3,2,1,0:T(8,128)}) custom-call(f32[256,128]{1,0:T(8,128)S(1)} %get-tuple-element.18.refs_0_, f32[256,128]{1,0:T(8,128)S(1)} %get-tuple-element.19.refs_1_, ...), custom_call_target="tpu_custom_call" | custom-call | tf_op jit(solution)/shard_map/pallas_call | solution.py:425
